TPU v7x, 128 devices: a whole 4x4x4 slice. The times are simulated.
128 devices in a mesh: particle: 8 (over z, core), lat: 2 (over y_lo), lon: 8 (over x, y_hi).
Axes of the slice: x: 4, y: 4 (y_hi: 2, y_lo: 2; y = y_hi * 2 + y_lo), z: 4, core: 2. Of those that a mesh axis runs over, the one named last changes fastest.
Arguments:
- states: float32 [32, 3, 3, 256, 1024], P('particle', None, None, 'lat', 'lon'), may hold values from -6 to 6
- ancestors: int32 [32], replicated, may hold values from 0 to 31
- coriolis: float32 [256], P('lat'), may hold values from -1 to 1
- depth: float32 [256, 1024], P('lat', 'lon'), may hold values from 0.5 to 2
Outputs:
- forecast: float32 [32, 3, 3, 256, 1024], P('particle', None, None, 'lat', 'lon')
All inputs are finite; a program needn't handle non-finite values.
Results may differ from a plain program's by a relative error of at most 0.00023.
Values sent between devices are 32-bit elements; how exact they have to be, the bound alone decides.
A program may use at most 128 MiB of HBM per device.

v0:
```python
import functools

import jax
import jax.numpy as jnp
from jax import lax
from jax.experimental import pallas as pl
from jax.experimental.pallas import tpu as pltpu
from jax.sharding import PartitionSpec as P

STEPS = 8
DT = 0.25
H_TOP = 1.0
H_MID = 0.8
REDUCED_GRAVITY_A = 0.2
REDUCED_GRAVITY_B = 0.2

MESH = pl.DeviceIdType.MESH
MEMBERS = 4
FIELDS = 9
SIDE = 128
HALO = 8
ROWS = SIDE + HALO
GROUPS = ROWS // 8
ROUNDS = (4, 5, 6)
MOST = ROUNDS[-1]
PLAN_SENDS = 8
PLAN_OUTS = PLAN_SENDS + 3 * MOST
PLAN_SIZE = PLAN_OUTS + 4 * MEMBERS


def padded(cells, sides, width, closed):
    for axis, dim in sides:
        count = lax.axis_size(axis)
        ends = count if closed else count - 1
        head = lax.slice_in_dim(cells, 0, width, axis=dim)
        tail = lax.slice_in_dim(cells, cells.shape[dim] - width, cells.shape[dim], axis=dim)
        cells = jnp.concatenate(
            [
                lax.ppermute(tail, axis, [(i, (i + 1) % count) for i in range(ends)]),
                cells,
                lax.ppermute(head, axis, [((i + 1) % count, i) for i in range(ends)]),
            ],
            axis=dim,
        )
    return cells


def pressure(thick):
    first = thick[..., 0, :, :] + thick[..., 1, :, :] + thick[..., 2, :, :]
    second = first + REDUCED_GRAVITY_A * (thick[..., 1, :, :] + thick[..., 2, :, :])
    third = second + REDUCED_GRAVITY_B * thick[..., 2, :, :]
    return jnp.stack([first, second, third], axis=-3)


def advance_in_time(height, east, north, fcor, bottom):
    layers = jnp.stack([jnp.full_like(bottom, H_TOP), jnp.full_like(bottom, H_MID), bottom], axis=0)
    layers = layers[:, 1:-1, 1:-1]
    diverg = (
        east[..., 1:-1, 2:]
        - east[..., 1:-1, 1:-1]
        + (north[..., 2:, 1:-1] - north[..., 1:-1, 1:-1])
    )
    newh = height[..., 1:-1, 1:-1] - DT * layers * diverg
    montg = pressure(newh)
    grad_x = montg[..., 1:-1, 1:-1] - montg[..., 1:-1, :-2]
    grad_y = montg[..., 1:-1, 1:-1] - montg[..., :-2, 1:-1]
    vbar = 0.25 * (
        north[..., 2:-2, 2:-2]
        + north[..., 3:-1, 2:-2]
        + north[..., 2:-2, 1:-3]
        + north[..., 3:-1, 1:-3]
    )
    ubar = 0.25 * (
        east[..., 2:-2, 2:-2]
        + east[..., 1:-3, 2:-2]
        + east[..., 2:-2, 3:-1]
        + east[..., 1:-3, 3:-1]
    )
    fcen = fcor[2:-2, 2:-2]
    neweast = east[..., 2:-2, 2:-2] + DT * (fcen * vbar - grad_x)
    updated_north_velocity = north[..., 2:-2, 2:-2] - DT * (fcen * ubar + grad_y)
    return (newh[..., 1:-1, 1:-1], neweast, updated_north_velocity)


def extend(stacked, width):
    wide = padded(stacked, (("lon", 2),), width, True)
    return padded(wide, (("lat", 1),), width, False)


def gather_all(states, ancestors, coriolis, depth):
    count = states.shape[0]
    ny, nx = depth.shape
    fcor = jnp.broadcast_to(coriolis[:, None], depth.shape)
    statics = extend(jnp.stack([fcor, depth], axis=0), 2)
    wanted = lax.dynamic_slice_in_dim(ancestors, lax.axis_index("particle") * count, count)
    piece = lax.all_gather(states, "particle", axis=0, tiled=True)
    current = jnp.take(piece, wanted, axis=0, mode="clip")
    rows = lax.axis_index("lat") * ny + jnp.arange(ny)
    wall = (rows > 0).astype(jnp.float32)[:, None]

    def step(_, current):
        wide = extend(current.reshape(count * 9, ny, nx), 2).reshape(count, 3, 3, ny + 4, nx + 4)
        height, east, north = advance_in_time(wide[:, 0], wide[:, 1], wide[:, 2], statics[0], statics[1])
        return jnp.stack([height, east, north * wall], axis=1)

    return lax.fori_loop(0, STEPS, step, current)


def ones8(v):
    v = v - ((v >> 1) & 85)
    v = (v & 51) + ((v >> 2) & 51)
    return (v + (v >> 4)) & 15


def place8(bit):
    odd = jnp.where((bit & 0xAA) != 0, 1, 0)
    two = jnp.where((bit & 0xCC) != 0, 2, 0)
    return odd + two + jnp.where((bit & 0xF0) != 0, 4, 0)


def routes(anc):
    one = jnp.int32(1)
    need = [jnp.int32(0)] * 4
    for p in range(32):
        need[p // 8] = need[p // 8] | (one << anc[p])
    ahead = [[(need[(c + k) % 4] >> (8 * c)) & 255 for c in range(4)] for k in range(4)]
    n1, n2, n3 = ahead[1], ahead[2], ahead[3]
    long_up = [n2[c] & n1[c] & ~n3[c] for c in range(4)]
    long_dn = [n2[c] & n3[c] & ~n1[c] for c in range(4)]
    either = [n2[c] & ~(n1[c] ^ n3[c]) for c in range(4)]
    up = [ones8(n1[c]) + ones8(long_up[(c - 1) % 4]) for c in range(4)]
    dn = [ones8(n3[c]) + ones8(long_dn[(c + 1) % 4]) for c in range(4)]
    for b in range(8):
        for c in range(4):
            e, w = (c + 1) % 4, (c - 1) % 4
            asked = (either[c] >> b) & 1
            extra = 1 - ((n1[c] >> b) & 1)
            by_up = jnp.maximum(up[e] + 1, up[c] + extra)
            by_dn = jnp.maximum(dn[w] + 1, dn[c] + extra)
            plus = jnp.where(by_up <= by_dn, asked, 0)
            minus = asked - plus
            up[e] = up[e] + plus
            up[c] = up[c] + plus * extra
            dn[w] = dn[w] + minus
            dn[c] = dn[c] + minus * extra
            long_up[c] = long_up[c] | (plus << b)
            long_dn[c] = long_dn[c] | (minus << b)
    own, passed = [], []
    rounds = jnp.int32(0)
    left = jnp.int32(0)
    for d in range(2):
        far = list((long_up, long_dn)[d])
        near = [(n1, n3)[d][c] & ~far[c] for c in range(4)]
        queue = [jnp.int32(0)] * 4
        before = [jnp.int32(0)] * 4
        for r in range(MOST):
            sent, relayed, fresh = [], [], []
            busy = jnp.int32(0)
            for c in range(4):
                may = (15 << (4 * d)) if r == 0 else 255
                f = far[c] & may
                pick = jnp.where(f != 0, f, near[c] & may)
                o = pick & (-pick)
                t = jnp.where(o != 0, 0, queue[c] & (-queue[c]))
                far[c] = far[c] & ~o
                near[c] = near[c] & ~o
                queue[c] = queue[c] & ~t
                sent.append(o)
                relayed.append(t)
                fresh.append(jnp.where(f != 0, o, 0))
                busy = busy | o | t
            own.append(sent)
            passed.append(relayed)
            rounds = jnp.where(busy != 0, jnp.maximum(rounds, r + 1), rounds)
            for c in range(4):
                source = (c - 1) % 4 if d == 0 else (c + 1) % 4
                queue[c] = queue[c] | before[source]
            before = fresh
        for c in range(4):
            left = left | far[c] | near[c] | queue[c] | before[c]
    return own, passed, rounds, left


def plan_kernel(anc_ref, cor_ref, depth_ref, plan_ref, stat_ref, own_ref, passed_ref):
    particle = lax.axis_index("particle")
    chip, core = particle // 2, lax.rem(particle, 2)
    anc = [anc_ref[p] for p in range(32)]
    own, passed, rounds, left = routes(anc)
    for i in range(2 * MOST):
        for c in range(4):
            own_ref[i * 4 + c] = own[i][c]
            passed_ref[i * 4 + c] = passed[i][c]
    variant = jnp.int32(0)
    for i, r in enumerate(ROUNDS[:-1]):
        variant = jnp.where(rounds > r, i + 1, variant)
    plan_ref[0] = jnp.where(left != 0, len(ROUNDS), variant)

    firsts = [place8(own_ref[(d * MOST) * 4 + chip] >> (4 * d)) for d in range(2)]

    def slot_of(side, local):
        first = jnp.where(side == 0, firsts[0], firsts[1])
        return jnp.where(local == 0, first, jnp.where(local == first, 0, local))

    def pool_of(bit):
        return (bit >> 2) * 4 + slot_of(bit >> 2, bit & 3)

    for k in range(MEMBERS):
        plan_ref[1 + k] = slot_of(core, jnp.int32(k))
    behind = lax.rem(chip + 3 + 2 * core, 4)
    for r in range(1, MOST):
        at = (core * MOST + r) * 4 + chip
        relay = passed_ref[at]
        plan_ref[PLAN_SENDS + 3 * r] = pool_of(place8(own_ref[at]))
        plan_ref[PLAN_SENDS + 3 * r + 1] = jnp.where(relay != 0, 1, 0)
        found = jnp.int32(0)
        for q in range(r - 1):
            found = jnp.where(own_ref[(core * MOST + q) * 4 + behind] == relay, q, found)
        plan_ref[PLAN_SENDS + 3 * r + 2] = found
    for i in range(MEMBERS):
        m = anc_ref[particle * MEMBERS + i]
        bit = m & 7
        mask = jnp.int32(1) << bit
        away = lax.rem((m >> 3) - chip + 4, 4)
        way, when = jnp.int32(0), jnp.int32(0)
        for d in range(2):
            source = lax.rem(chip + (3 if d == 0 else 1), 4)
            direct = away == (3 if d == 0 else 1)
            for r in range(MOST):
                at = (d * MOST + r) * 4 + source
                hit = (direct & (own_ref[at] == mask)) | ((away == 2) & (passed_ref[at] == mask))
                way = jnp.where(hit, d, way)
                when = jnp.where(hit, r, when)
        plan_ref[PLAN_OUTS + 4 * i] = jnp.where(away == 0, 1, 0)
        plan_ref[PLAN_OUTS + 4 * i + 1] = pool_of(bit)
        plan_ref[PLAN_OUTS + 4 * i + 2] = way
        plan_ref[PLAN_OUTS + 4 * i + 3] = when

    stat_ref[0] = DT * depth_ref[...]
    stat_ref[1] = jnp.transpose(jnp.broadcast_to((DT * 0.25) * cor_ref[...], (SIDE, SIDE)))


def main_kernel(
    rounds, plan, states, stat, out,
    raw, st, st_edge, st_land, pack_w, pack_e, land_w, land_e, edge, edge_land,
    tall, wm, ws, wd, wds, wf, pool, recv, stage, done,
    in_sem, halo_send, halo_recv, mir_send, mir_recv, z_send, z_recv, fwd_send, fwd_recv, out_sem,
):
    particle, lat, lon = lax.axis_index("particle"), lax.axis_index("lat"), lax.axis_index("lon")
    chip, core = particle // 2, lax.rem(particle, 2)
    lat2 = 1 - lat
    east, west = lax.rem(lon + 1, 8), lax.rem(lon + 7, 8)
    mate = chip * 2 + 1 - core
    ahead = lax.rem(chip + 1 + 2 * core, 4) * 2 + core
    behind = lax.rem(chip + 3 + 2 * core, 4) * 2 + core

    load = pltpu.make_async_copy(states, raw, in_sem.at[0])
    load.start()
    load_stat = pltpu.make_async_copy(stat, st.at[:, pl.ds(0, SIDE), :], in_sem.at[1])
    load_stat.start()
    barrier = pltpu.get_barrier_semaphore()
    everyone = (
        (particle, lat, east), (particle, lat, west), (particle, lat2, lon), (particle, lat2, east),
        (particle, lat2, west), (mate, lat, lon), (ahead, lat, lon), (behind, lat, lon),
    )
    for who in everyone:
        pl.semaphore_signal(barrier, inc=1, device_id=who, device_id_type=MESH)

    lane = lax.broadcasted_iota(jnp.int32, (8, SIDE), 1)
    sub = lax.broadcasted_iota(jnp.int32, (8, SIDE), 0)
    edge_row = pl.multiple_of((SIDE - HALO) * lat2, HALO)

    def pack(k):
        m = plan[1 + k]

        def rows(i, _):
            at = pl.multiple_of(i * 8, 8)
            to_e = jnp.zeros((8, SIDE), jnp.float32)
            to_w = jnp.zeros((8, SIDE), jnp.float32)
            for f in range(FIELDS + 1):
                x = raw[m, f, pl.ds(at, 8), :] if f < FIELDS else st[0, pl.ds(at, 8), :]
                x = pltpu.roll(x, 8 * f + 8, 1)
                to_e = jnp.where((lane >= 8 * f) & (lane < 8 * f + 8), x, to_e)
                to_w = jnp.where((lane >= 8 * f + 8) & (lane < 8 * f + 16), x, to_w)
            pack_w[k, pl.ds(at, 8), :] = to_e
            pack_e[k, pl.ds(at, 8), :] = to_w
            return 0

        lax.fori_loop(0, SIDE // 8, rows, 0)
        for f in range(FIELDS):
            edge[k, f] = raw[m, f, pl.ds(edge_row, HALO), :]

    def halo_copies(first, count, group):
        at = pl.ds(first, count)
        body, tail = pl.ds(0, SIDE), pl.ds(SIDE, HALO)
        rim = pl.ds(edge_row, HALO)
        ways = [
            (pack_w.at[at], land_w.at[at, body, :], (particle, lat, east)),
            (pack_e.at[at], land_e.at[at, body, :], (particle, lat, west)),
            (pack_w.at[at, rim, :], land_w.at[at, tail, :], (particle, lat2, east)),
            (pack_e.at[at, rim, :], land_e.at[at, tail, :], (particle, lat2, west)),
            (edge.at[at], edge_land.at[at], (particle, lat2, lon)),
        ]
        if group == 0:
            ways.append((st_edge, st_land, (particle, lat2, lon)))
        return [
            pltpu.make_async_remote_copy(
                src_ref=src, dst_ref=dst, send_sem=halo_send.at[group, i], recv_sem=halo_recv.at[group, i],
                device_id=who, device_id_type=MESH,
            )
            for i, (src, dst, who) in enumerate(ways)
        ]

    load_stat.wait()
    load.wait()
    pack(0)
    for i in range(2):
        st_edge[i] = st[i, pl.ds(edge_row, HALO), :]
    pl.semaphore_wait(barrier, len(everyone))
    halo_a = halo_copies(0, 1, 0)
    for copy in halo_a:
        copy.start()

    def pack_more(k, _):
        pack(k)
        return 0

    lax.fori_loop(1, MEMBERS, pack_more, 0)
    halo_b = halo_copies(1, MEMBERS - 1, 1)
    for copy in halo_b:
        copy.start()

    def shifted(tiles, offs, left):
        turned = [pltpu.roll(x, SIDE - 1 if left else 1, 1) for x in tiles]
        strip = turned[-1]
        result = []
        for x, off in zip(turned[:-1], offs):
            here = lane == ((off - 1) % SIDE if left else off)
            result.append(jnp.where(here, strip, x))
            strip = jnp.where(here, x, strip)
        return result + [strip]

    def strided(j):
        return pl.ds(j, 8, stride=GROUPS)

    no_north = (sub == 7) & (lat == 1)
    wall = (sub == 0) & (lat == 0)

    def advance(first, offs):
        n = len(offs)
        tiles = range(n + 1)

        for g, off in enumerate(offs):
            k = first + g
            m = plan[1 + k]

            def fill(f, _):
                tall[f, pl.ds(0, SIDE), :] = raw[m, f]
                tall[f, pl.ds(SIDE, HALO), :] = edge_land[k, f]
                for j in range(GROUPS):
                    x = tall[f, strided(j), :]
                    wm[g, f, j] = pltpu.roll(x, off, 1) if off else x
                return 0

            lax.fori_loop(0, FIELDS, fill, 0)
            for j in range(GROUPS):
                x = st[0, strided(j), :]
                wd[g, j] = pltpu.roll(x, off, 1) if off else x

        def fill_strip(j, _):
            lw = [land_w[first + g, strided(j), :] for g in range(n)]
            le = [land_e[first + g, strided(j), :] for g in range(n)]
            for f in range(FIELDS + 1):
                total = None
                for g, off in enumerate(offs):
                    x = jnp.where((lane >= 8 * f) & (lane < 8 * f + 8), lw[g], le[g])
                    turn = (off - 8 - 8 * f) % SIDE
                    x = pltpu.roll(x, turn, 1) if turn else x
                    total = x if g == 0 else jnp.where((lane >= off - 16) & (lane < off + 16), x, total)
                if f < FIELDS:
                    ws[f, j] = total
                else:
                    wds[j] = total
            return 0

        lax.fori_loop(0, GROUPS, fill_strip, 0)

        def get(f, j):
            return [wm[g, f, j] for g in range(n)] + [ws[f, j]]

        def put(f, j, values):
            for g in range(n):
                wm[g, f, j] = values[g]
            ws[f, j] = values[n]

        def front(j, north):
            rot = wf[j]
            bottom = [wd[g, j] for g in range(n)] + [wds[j]]
            high, sums = [], []
            for l in range(3):
                h, u, v = get(l, j), get(3 + l, j), get(6 + l, j)
                right = shifted(u, offs, True)
                sums.append([u[t] + right[t] for t in tiles])
                thick = [(DT * H_TOP), (DT * H_MID), None][l]
                new = []
                for t in tiles:
                    div = (right[t] - u[t]) + (north[l][t] - v[t])
                    new.append(h[t] - (bottom[t] if thick is None else thick) * div)
                high.append(new)
                put(l, j, new)
            two = [high[1][t] + high[2][t] for t in tiles]
            m0 = [high[0][t] + two[t] for t in tiles]
            m1 = [m0[t] + REDUCED_GRAVITY_A * two[t] for t in tiles]
            m2 = [m1[t] + REDUCED_GRAVITY_B * high[2][t] for t in tiles]
            press = [[DT * m[t] for t in tiles] for m in (m0, m1, m2)]
            for l in range(3):
                u, v = get(3 + l, j), get(6 + l, j)
                turn = [rot * (v[t] + north[l][t]) for t in tiles]
                back = shifted([turn[t] + press[l][t] for t in tiles], offs, False)
                put(3 + l, j, [u[t] + ((turn[t] - press[l][t]) + back[t]) for t in tiles])
            return press, sums

        def finish(j, now, last):
            rot = wf[j]
            press, sums = now
            press0, sums0 = last
            for l in range(3):
                v = get(6 + l, j)
                new = [
                    v[t] - (rot * (sums[l][t] + sums0[l][t]) + (press[l][t] - press0[l][t])) for t in tiles
                ]
                if j == 0:
                    new = [jnp.where(wall, 0.0, x) for x in new]
                put(6 + l, j, new)

        def step(_, carry):
            end = GROUPS - 1
            north = [[pltpu.roll(x, 7, 0) for x in get(6 + l, 0)] for l in range(3)]
            tail = front(end, north)
            last = [[[pltpu.roll(x, 1, 0) for x in layer] for layer in part] for part in tail]
            for j in range(end):
                north = [get(6 + l, j + 1) for l in range(3)]
                if j == (SIDE - 1) - 7 * GROUPS:
                    north = [[jnp.where(no_north, 0.0, x) for x in layer] for layer in north]
                now = front(j, north)
                finish(j, now, last)
                last = now
            finish(end, tail, last)
            return carry

        lax.fori_loop(0, STEPS, step, 0)

        for g, off in enumerate(offs):
            slot = core * MEMBERS + first + g

            def drain(f, _):
                for j in range(GROUPS):
                    x = wm[g, f, j]
                    pool[slot, f, strided(j), :] = pltpu.roll(x, SIDE - off, 1) if off else x
                return 0

            lax.fori_loop(0, FIELDS, drain, 0)

    def mirror(first, count, i):
        part = pool.at[pl.ds(core * MEMBERS + first, count), :, pl.ds(0, SIDE), :]
        return pltpu.make_async_remote_copy(
            src_ref=part, dst_ref=part, send_sem=mir_send.at[i], recv_sem=mir_recv.at[i],
            device_id=(mate, lat, lon), device_id_type=MESH,
        )

    def hop(r):
        src = stage.at[r] if r else pool.at[core * MEMBERS, :, pl.ds(0, SIDE), :]
        return pltpu.make_async_remote_copy(
            src_ref=src, dst_ref=recv.at[core, r], send_sem=z_send.at[r], recv_sem=z_recv.at[r],
            device_id=(ahead, lat, lon), device_id_type=MESH,
        )

    def forward(r):
        return pltpu.make_async_remote_copy(
            src_ref=recv.at[core, r], dst_ref=recv.at[core, r], send_sem=fwd_send.at[r], recv_sem=fwd_recv.at[r],
            device_id=(mate, lat, lon), device_id_type=MESH,
        )

    for copy in halo_a:
        copy.wait_recv()
    for i in range(2):
        st[i, pl.ds(SIDE, HALO), :] = st_land[i]
    for j in range(GROUPS):
        wf[j] = st[1, strided(j), :]
    advance(0, (0,))
    hops = [hop(r) for r in range(rounds)]
    forwards = [forward(r) for r in range(rounds)]
    hops[0].start()
    mirrors = [mirror(0, 1, 0), mirror(1, MEMBERS - 1, 1)]
    mirrors[0].start()

    for copy in halo_b:
        copy.wait_recv()
    advance(1, (0, 32, 64))
    mirrors[1].start()
    for copy in mirrors:
        copy.wait_recv()

    for r in range(1, rounds):
        if r >= 2:
            hops[r - 2].wait_recv()
            forwards[r - 2].start()
            hops[r - 2].wait_send()
        own, relay, which = (plan[PLAN_SENDS + 3 * r + i] for i in range(3))

        def fill_stage(f, _):
            x = pool[own, f, pl.ds(0, SIDE), :]
            for q in range(r - 1):
                x = jnp.where((relay == 1) & (which == q), recv[core, q, f], x)
            stage[r, f] = x
            return 0

        lax.fori_loop(0, FIELDS, fill_stage, 0)
        hops[r].start()
    for r in range(max(0, rounds - 2), rounds):
        hops[r].wait_recv()
        forwards[r].start()
        hops[r].wait_send()
    for copy in forwards:
        copy.wait()
    for copy in mirrors:
        copy.wait_send()
    for copy in halo_a + halo_b:
        copy.wait_send()

    writes = []
    for i in range(MEMBERS):
        here, at, way, when = (plan[PLAN_OUTS + 4 * i + e] for e in range(4))

        def choose(f, _):
            done[i, f] = jnp.where(here == 1, pool[at, f, pl.ds(0, SIDE), :], recv[way, when, f])
            return 0

        lax.fori_loop(0, FIELDS, choose, 0)
        write = pltpu.make_async_copy(done.at[i], out.at[i], out_sem.at[i])
        write.start()
        writes.append(write)
    for write in writes:
        write.wait()


def main_call(rounds, cid):
    f32 = jnp.float32
    tile = (FIELDS, SIDE, SIDE)
    scratch = [
        pltpu.VMEM((MEMBERS, *tile), f32),
        pltpu.VMEM((2, ROWS, SIDE), f32),
        pltpu.VMEM((2, HALO, SIDE), f32),
        pltpu.VMEM((2, HALO, SIDE), f32),
        pltpu.VMEM((MEMBERS, SIDE, SIDE), f32),
        pltpu.VMEM((MEMBERS, SIDE, SIDE), f32),
        pltpu.VMEM((MEMBERS, ROWS, SIDE), f32),
        pltpu.VMEM((MEMBERS, ROWS, SIDE), f32),
        pltpu.VMEM((MEMBERS, FIELDS, HALO, SIDE), f32),
        pltpu.VMEM((MEMBERS, FIELDS, HALO, SIDE), f32),
        pltpu.VMEM((FIELDS, ROWS, SIDE), f32),
        pltpu.VMEM((3, FIELDS, GROUPS, 8, SIDE), f32),
        pltpu.VMEM((FIELDS, GROUPS, 8, SIDE), f32),
        pltpu.VMEM((3, GROUPS, 8, SIDE), f32),
        pltpu.VMEM((GROUPS, 8, SIDE), f32),
        pltpu.VMEM((GROUPS, 8, SIDE), f32),
        pltpu.VMEM((2 * MEMBERS, FIELDS, ROWS, SIDE), f32),
        pltpu.VMEM((2, rounds, *tile), f32),
        pltpu.VMEM((rounds, *tile), f32),
        pltpu.VMEM((MEMBERS, *tile), f32),
        pltpu.SemaphoreType.DMA((2,)),
        pltpu.SemaphoreType.DMA((2, 6)),
        pltpu.SemaphoreType.DMA((2, 6)),
        pltpu.SemaphoreType.DMA((2,)),
        pltpu.SemaphoreType.DMA((2,)),
        pltpu.SemaphoreType.DMA((rounds,)),
        pltpu.SemaphoreType.DMA((rounds,)),
        pltpu.SemaphoreType.DMA((rounds,)),
        pltpu.SemaphoreType.DMA((rounds,)),
        pltpu.SemaphoreType.DMA((MEMBERS,)),
    ]
    return pl.pallas_call(
        functools.partial(main_kernel, rounds),
        out_shape=jax.ShapeDtypeStruct((MEMBERS, *tile), f32),
        in_specs=[
            pl.BlockSpec(memory_space=pltpu.SMEM),
            pl.BlockSpec(memory_space=pl.ANY),
            pl.BlockSpec(memory_space=pl.ANY),
        ],
        out_specs=pl.BlockSpec(memory_space=pl.ANY),
        scratch_shapes=scratch,
        compiler_params=pltpu.CompilerParams(
            collective_id=cid, has_side_effects=True, vmem_limit_bytes=50 * 2**20
        ),
        name=f"cycle_{rounds}",
    )


def body(states, ancestors, coriolis, depth):
    plan, stat = pl.pallas_call(
        plan_kernel,
        out_shape=(
            jax.ShapeDtypeStruct((PLAN_SIZE,), jnp.int32),
            jax.ShapeDtypeStruct((2, SIDE, SIDE), jnp.float32),
        ),
        in_specs=[
            pl.BlockSpec(memory_space=pltpu.SMEM),
            pl.BlockSpec(memory_space=pltpu.VMEM),
            pl.BlockSpec(memory_space=pltpu.VMEM),
        ],
        out_specs=(pl.BlockSpec(memory_space=pltpu.SMEM), pl.BlockSpec(memory_space=pltpu.VMEM)),
        scratch_shapes=[pltpu.SMEM((8 * MOST,), jnp.int32)] * 2,
        name="plan",
    )(ancestors, coriolis.reshape(1, SIDE), depth)

    def by_kernel(rounds, cid):
        def run(states, ancestors, coriolis, depth, plan, stat):
            flat = states.reshape(MEMBERS, FIELDS, SIDE, SIDE)
            return main_call(rounds, cid)(plan, flat, stat).reshape(states.shape)

        return run

    def by_gather(states, ancestors, coriolis, depth, plan, stat):
        return gather_all(states, ancestors, coriolis, depth)

    branches = [by_kernel(r, i) for i, r in enumerate(ROUNDS)] + [by_gather]
    return lax.switch(plan[0], branches, states, ancestors, coriolis, depth, plan, stat)


def solution(mesh):
    in_specs = (P("particle", None, None, "lat", "lon"), P(), P("lat"), P("lat", "lon"))
    out_specs = P("particle", None, None, "lat", "lon")
    return jax.shard_map(body, mesh=mesh, in_specs=in_specs, out_specs=out_specs, check_vma=False)
```

profile of v0, /device:TPU:1, one launch (start us, length us, event | category | flops | bytes accessed | tf_op | source)
XLA Modules:
  0.0 96.1 jit_solution(17914323212270601673)
XLA Ops:
  6.5 2.5 %plan.1 = (s32[42]{0:T(128)S(1)}, f32[2,128,128]{2,1,0:T(8,128)S(1)}) custom-call(s32[32]{0:T(128)} %anc_ref.1, f32[1,128]{1,0:T(1,128)} %bitcast.62, f32[128,128]{1,0:T(8,128)} %depth_ref.1), custom_call_target="tpu_custom_call" | custom-call | tf_op jit(solution)/shard_map/plan/pallas_call | solution.py:599
  9.1 78.8 %conditional.1 = (f32[4,3,3,128,128]{4,3,2,1,0:T(8,128)S(1)}) conditional(s32[]{:T(128)} %bitcast.8, (f32[4,3,3,128,128]{4,3,2,1,0:T(8,128)}, s32[42]{0:T(128)S(1)}, f32[2,128,128]{2,1,0:T(8,128)S(1)}) %tuple.21, (f32[4,3,3,128,128]{4,3,2,1,0:T(8,128)}, s32[42]{0:T(128)S(1)}, f32[2,128,128]{2,1,0:T(8,128)S(1)}) %tuple.21, ...), branch_computations={%region_0.0_spmd, %region_1.0_spmd, %region_2.0_spmd, %region_3.6_... | conditional | flops 9259496 | bytes 122663120 | solution.py:626
  9.1 78.5 %cycle_5.1 = f32[4,9,128,128]{3,2,1,0:T(8,128)S(1)} custom-call(s32[42]{0:T(128)S(1)} %get-tuple-element.55.plan, f32[4,9,128,128]{3,2,1,0:T(8,128)} %bitcast.53, f32[2,128,128]{2,1,0:T(8,128)S(1)} %get-tuple-element.57.stat), custom_call_target="tpu_custom_call" | custom-call | tf_op jit(solution)/shard_map/cond/branch_1_fun/cycle_5/pallas_call | solution.py:618
  87.8 1.4 %copy.62 = f32[4,3,3,128,128]{4,3,2,1,0:T(8,128)} copy(f32[4,3,3,128,128]{4,3,2,1,0:T(8,128)S(1)} %get-tuple-element.104) | data formatting | bytes 4718592
where the time goes:
time: 96.3 us; the launch traced here: 96.1 us
  Pallas kernels  81 us (84%)
  between operations  13.4 us (14%)
  local copies, waits for them, and re-layouts  1.41 us (1%)
    pallas_call x1, Pallas kernels, run(): return main_call(rounds, cid)(plan, flat, stat).reshape(states.shape)  78.5 us
    pallas_call x1, Pallas kernels, body(): pl.pallas_call(plan_kernel, out_shape=(jax.ShapeDtypeStruct((PLAN_SIZE,),...  2.49 us

commit v1 on v0

--- a/solution.py
+++ b/solution.py
@@ -21,6 +21,7 @@
 HALO = 8
 ROWS = SIDE + HALO
 GROUPS = ROWS // 8
+WAVES = ((0, 1), (1, 1), (2, 2))
 ROUNDS = (4, 5, 6)
 MOST = ROUNDS[-1]
 PLAN_SENDS = 8
@@ -93,8 +94,16 @@
     fcor = jnp.broadcast_to(coriolis[:, None], depth.shape)
     statics = extend(jnp.stack([fcor, depth], axis=0), 2)
     wanted = lax.dynamic_slice_in_dim(ancestors, lax.axis_index("particle") * count, count)
-    piece = lax.all_gather(states, "particle", axis=0, tiled=True)
-    current = jnp.take(piece, wanted, axis=0, mode="clip")
+    me, devices = lax.axis_index("particle"), lax.axis_size("particle")
+
+    def turn(k, carry):
+        piece, current = carry
+        owner = lax.rem(me - k + devices, devices)
+        here = (wanted // count == owner)[:, None, None, None, None]
+        current = jnp.where(here, jnp.take(piece, wanted % count, axis=0, mode="clip"), current)
+        return lax.ppermute(piece, "particle", [(i, (i + 1) % devices) for i in range(devices)]), current
+
+    current = lax.fori_loop(0, devices, turn, (states, jnp.zeros_like(states)))[1]
     rows = lax.axis_index("lat") * ny + jnp.arange(ny)
     wall = (rows > 0).astype(jnp.float32)[:, None]
 
@@ -145,67 +154,93 @@
             dn[c] = dn[c] + minus * extra
             long_up[c] = long_up[c] | (plus << b)
             long_dn[c] = long_dn[c] | (minus << b)
-    own, passed = [], []
+    far = [long_up, long_dn]
+    near = [[(n1, n3)[d][c] & ~far[d][c] for c in range(4)] for d in range(2)]
+    queue = [[jnp.int32(0)] * 4 for _ in range(2)]
+    before = [[jnp.int32(0)] * 4 for _ in range(2)]
+    own, passed = {}, {}
     rounds = jnp.int32(0)
+    early = [[15, 240] for _ in range(4)]
+    first, second = None, None
+    for r in range(MOST):
+        busy = jnp.int32(0)
+        for d in range(2):
+            fresh = []
+            for c in range(4):
+                may = (15 << (4 * d)) if r == 0 else (early[c] if r == 1 else 255)
+                f = far[d][c] & may
+                pick = jnp.where(f != 0, f, near[d][c] & may)
+                o = pick & (-pick)
+                t = jnp.where(o != 0, 0, queue[d][c] & (-queue[d][c]))
+                far[d][c] = far[d][c] & ~o
+                near[d][c] = near[d][c] & ~o
+                queue[d][c] = queue[d][c] & ~t
+                own[d, r, c] = o
+                passed[d, r, c] = t
+                fresh.append(jnp.where(f != 0, o, 0))
+                busy = busy | o | t
+            for c in range(4):
+                source = (c - 1) % 4 if d == 0 else (c + 1) % 4
+                queue[d][c] = queue[d][c] | before[d][source]
+            before[d] = fresh
+        rounds = jnp.where(busy != 0, r + 1, rounds)
+        if r == 0:
+            first, second = {}, {}
+            for c in range(4):
+                for k in range(2):
+                    o = own[k, 0, c]
+                    first[c, k] = jnp.where(o != 0, o, 1 << (4 * k))
+                    rest = (15 << (4 * k)) & ~first[c, k]
+                    a = (far[0][c] | far[1][c]) & rest
+                    b = (near[0][c] | near[1][c]) & rest
+                    pick = jnp.where(a != 0, a, jnp.where(b != 0, b, rest))
+                    second[c, k] = pick & (-pick)
+                early[c] = first[c, 0] | first[c, 1] | second[c, 0] | second[c, 1]
     left = jnp.int32(0)
     for d in range(2):
-        far = list((long_up, long_dn)[d])
-        near = [(n1, n3)[d][c] & ~far[c] for c in range(4)]
-        queue = [jnp.int32(0)] * 4
-        before = [jnp.int32(0)] * 4
-        for r in range(MOST):
-            sent, relayed, fresh = [], [], []
-            busy = jnp.int32(0)
-            for c in range(4):
-                may = (15 << (4 * d)) if r == 0 else 255
-                f = far[c] & may
-                pick = jnp.where(f != 0, f, near[c] & may)
-                o = pick & (-pick)
-                t = jnp.where(o != 0, 0, queue[c] & (-queue[c]))
-                far[c] = far[c] & ~o
-                near[c] = near[c] & ~o
-                queue[c] = queue[c] & ~t
-                sent.append(o)
-                relayed.append(t)
-                fresh.append(jnp.where(f != 0, o, 0))
-                busy = busy | o | t
-            own.append(sent)
-            passed.append(relayed)
-            rounds = jnp.where(busy != 0, jnp.maximum(rounds, r + 1), rounds)
-            for c in range(4):
-                source = (c - 1) % 4 if d == 0 else (c + 1) % 4
-                queue[c] = queue[c] | before[source]
-            before = fresh
         for c in range(4):
-            left = left | far[c] | near[c] | queue[c] | before[c]
-    return own, passed, rounds, left
-
-
-def plan_kernel(anc_ref, cor_ref, depth_ref, plan_ref, stat_ref, own_ref, passed_ref):
+            left = left | far[d][c] | near[d][c] | queue[d][c] | before[d][c]
+    return own, passed, first, second, rounds, left
+
+
+def plan_kernel(anc_ref, cor_ref, depth_ref, plan_ref, stat_ref, own_ref, passed_ref, order_ref):
     particle = lax.axis_index("particle")
     chip, core = particle // 2, lax.rem(particle, 2)
     anc = [anc_ref[p] for p in range(32)]
-    own, passed, rounds, left = routes(anc)
-    for i in range(2 * MOST):
+    own, passed, first, second, rounds, left = routes(anc)
+    for d in range(2):
+        for r in range(MOST):
+            for c in range(4):
+                own_ref[(d * MOST + r) * 4 + c] = own[d, r, c]
+                passed_ref[(d * MOST + r) * 4 + c] = passed[d, r, c]
         for c in range(4):
-            own_ref[i * 4 + c] = own[i][c]
-            passed_ref[i * 4 + c] = passed[i][c]
+            order_ref[(c * 2 + d) * 2] = first[c, d]
+            order_ref[(c * 2 + d) * 2 + 1] = second[c, d]
     variant = jnp.int32(0)
     for i, r in enumerate(ROUNDS[:-1]):
         variant = jnp.where(rounds > r, i + 1, variant)
     plan_ref[0] = jnp.where(left != 0, len(ROUNDS), variant)
 
-    firsts = [place8(own_ref[(d * MOST) * 4 + chip] >> (4 * d)) for d in range(2)]
-
-    def slot_of(side, local):
-        first = jnp.where(side == 0, firsts[0], firsts[1])
-        return jnp.where(local == 0, first, jnp.where(local == first, 0, local))
+    firsts = [place8(order_ref[(chip * 2 + k) * 2]) & 3 for k in range(2)]
+    seconds = [place8(order_ref[(chip * 2 + k) * 2 + 1]) & 3 for k in range(2)]
 
     def pool_of(bit):
-        return (bit >> 2) * 4 + slot_of(bit >> 2, bit & 3)
-
+        side, local = bit >> 2, bit & 3
+        one = jnp.where(side == 0, firsts[0], firsts[1])
+        two = jnp.where(side == 0, seconds[0], seconds[1])
+        rank = local - jnp.where(one < local, 1, 0) - jnp.where(two < local, 1, 0)
+        slot = jnp.where(local == one, 0, jnp.where(local == two, 1, 2 + rank))
+        return (slot >> 1) * 4 + side * 2 + (slot & 1)
+
+    one = jnp.where(core == 0, firsts[0], firsts[1])
+    two = jnp.where(core == 0, seconds[0], seconds[1])
+    third, fourth = jnp.int32(0), jnp.int32(0)
     for k in range(MEMBERS):
-        plan_ref[1 + k] = slot_of(core, jnp.int32(k))
+        fourth = jnp.where((one != k) & (two != k), k, fourth)
+        down = MEMBERS - 1 - k
+        third = jnp.where((one != down) & (two != down), down, third)
+    for k, local in enumerate((one, two, third, fourth)):
+        plan_ref[1 + k] = local
     behind = lax.rem(chip + 3 + 2 * core, 4)
     for r in range(1, MOST):
         at = (core * MOST + r) * 4 + chip
@@ -242,7 +277,7 @@
 def main_kernel(
     rounds, plan, states, stat, out,
     raw, st, st_edge, st_land, pack_w, pack_e, land_w, land_e, edge, edge_land,
-    tall, wm, ws, wd, wds, wf, pool, recv, stage, done,
+    tall, wm, ws, wd, wds, wf, pool_a, pool_b, recv, last, stage, done,
     in_sem, halo_send, halo_recv, mir_send, mir_recv, z_send, z_recv, fwd_send, fwd_recv, out_sem,
 ):
     particle, lat, lon = lax.axis_index("particle"), lax.axis_index("lat"), lax.axis_index("lon")
@@ -300,7 +335,7 @@
             (pack_e.at[at, rim, :], land_e.at[at, tail, :], (particle, lat2, west)),
             (edge.at[at], edge_land.at[at], (particle, lat2, lon)),
         ]
-        if group == 0:
+        if first == 0:
             ways.append((st_edge, st_land, (particle, lat2, lon)))
         return [
             pltpu.make_async_remote_copy(
@@ -316,8 +351,8 @@
     for i in range(2):
         st_edge[i] = st[i, pl.ds(edge_row, HALO), :]
     pl.semaphore_wait(barrier, len(everyone))
-    halo_a = halo_copies(0, 1, 0)
-    for copy in halo_a:
+    halos = [halo_copies(first, count, i) for i, (first, count) in enumerate(WAVES)]
+    for copy in halos[0]:
         copy.start()
 
     def pack_more(k, _):
@@ -325,8 +360,9 @@
         return 0
 
     lax.fori_loop(1, MEMBERS, pack_more, 0)
-    halo_b = halo_copies(1, MEMBERS - 1, 1)
-    for copy in halo_b:
+    for copy in halos[0]:
+        copy.wait_send()
+    for copy in halos[1] + halos[2]:
         copy.start()
 
     def shifted(tiles, offs, left):
@@ -392,65 +428,83 @@
                 wm[g, f, j] = values[g]
             ws[f, j] = values[n]
 
-        def front(j, north):
-            rot = wf[j]
+        def easts(j):
+            return [shifted(get(3 + l, j), offs, True) for l in range(3)]
+
+        def norths(j):
+            if j == GROUPS - 1:
+                return [[pltpu.roll(x, 7, 0) for x in get(6 + l, 0)] for l in range(3)]
+            north = [get(6 + l, j + 1) for l in range(3)]
+            if j == (SIDE - 1) - 7 * GROUPS:
+                north = [[jnp.where(no_north, 0.0, x) for x in layer] for layer in north]
+            return north
+
+        def middle(j, right):
+            rot, north = wf[j], norths(j)
             bottom = [wd[g, j] for g in range(n)] + [wds[j]]
-            high, sums = [], []
+            high, sums, turns = [], [], []
             for l in range(3):
                 h, u, v = get(l, j), get(3 + l, j), get(6 + l, j)
-                right = shifted(u, offs, True)
-                sums.append([u[t] + right[t] for t in tiles])
-                thick = [(DT * H_TOP), (DT * H_MID), None][l]
+                thick = [DT * H_TOP, DT * H_MID, None][l]
                 new = []
                 for t in tiles:
-                    div = (right[t] - u[t]) + (north[l][t] - v[t])
+                    div = (right[l][t] - u[t]) + (north[l][t] - v[t])
                     new.append(h[t] - (bottom[t] if thick is None else thick) * div)
-                high.append(new)
                 put(l, j, new)
+                high.append([DT * x for x in new])
+                turns.append([rot * (v[t] + north[l][t]) for t in tiles])
+                sums.append([u[t] + right[l][t] for t in tiles])
             two = [high[1][t] + high[2][t] for t in tiles]
             m0 = [high[0][t] + two[t] for t in tiles]
             m1 = [m0[t] + REDUCED_GRAVITY_A * two[t] for t in tiles]
             m2 = [m1[t] + REDUCED_GRAVITY_B * high[2][t] for t in tiles]
-            press = [[DT * m[t] for t in tiles] for m in (m0, m1, m2)]
+            press = [m0, m1, m2]
+            back = [shifted([turns[l][t] + press[l][t] for t in tiles], offs, False) for l in range(3)]
+            rest = [[turns[l][t] - press[l][t] for t in tiles] for l in range(3)]
+            return press, sums, rest, back
+
+        def set_u(j, now):
             for l in range(3):
-                u, v = get(3 + l, j), get(6 + l, j)
-                turn = [rot * (v[t] + north[l][t]) for t in tiles]
-                back = shifted([turn[t] + press[l][t] for t in tiles], offs, False)
-                put(3 + l, j, [u[t] + ((turn[t] - press[l][t]) + back[t]) for t in tiles])
-            return press, sums
-
-        def finish(j, now, last):
+                u = get(3 + l, j)
+                put(3 + l, j, [u[t] + (now[2][l][t] + now[3][l][t]) for t in tiles])
+
+        def set_v(j, now, south):
             rot = wf[j]
-            press, sums = now
-            press0, sums0 = last
             for l in range(3):
                 v = get(6 + l, j)
                 new = [
-                    v[t] - (rot * (sums[l][t] + sums0[l][t]) + (press[l][t] - press0[l][t])) for t in tiles
+                    v[t] - (rot * (now[1][l][t] + south[1][l][t]) + (now[0][l][t] - south[0][l][t]))
+                    for t in tiles
                 ]
                 if j == 0:
                     new = [jnp.where(wall, 0.0, x) for x in new]
                 put(6 + l, j, new)
 
         def step(_, carry):
-            end = GROUPS - 1
-            north = [[pltpu.roll(x, 7, 0) for x in get(6 + l, 0)] for l in range(3)]
-            tail = front(end, north)
-            last = [[[pltpu.roll(x, 1, 0) for x in layer] for layer in part] for part in tail]
-            for j in range(end):
-                north = [get(6 + l, j + 1) for l in range(3)]
-                if j == (SIDE - 1) - 7 * GROUPS:
-                    north = [[jnp.where(no_north, 0.0, x) for x in layer] for layer in north]
-                now = front(j, north)
-                finish(j, now, last)
-                last = now
-            finish(end, tail, last)
+            order = [GROUPS - 1] + list(range(GROUPS - 1))
+            right = {i: easts(order[i]) for i in range(2)}
+            made = {}
+            for i in range(GROUPS + 1):
+                if i + 2 < GROUPS:
+                    right[i + 2] = easts(order[i + 2])
+                if i < GROUPS:
+                    made[i] = middle(order[i], right.pop(i))
+                if i == 0:
+                    continue
+                set_u(order[i - 1], made[i - 1])
+                if i == 2:
+                    south = [[[pltpu.roll(x, 1, 0) for x in layer] for layer in part] for part in made[0][:2]]
+                    set_v(0, made[1], south)
+                elif i > 2:
+                    set_v(order[i - 1], made[i - 1], made[i - 2])
+            set_v(GROUPS - 1, made[0], made[GROUPS - 1])
             return carry
 
         lax.fori_loop(0, STEPS, step, 0)
 
         for g, off in enumerate(offs):
-            slot = core * MEMBERS + first + g
+            pool = pool_a if first < 2 else pool_b
+            slot = core * 2 + (first + g) % 2
 
             def drain(f, _):
                 for j in range(GROUPS):
@@ -460,87 +514,104 @@
 
             lax.fori_loop(0, FIELDS, drain, 0)
 
-    def mirror(first, count, i):
-        part = pool.at[pl.ds(core * MEMBERS + first, count), :, pl.ds(0, SIDE), :]
+    def remote(src, dst, send, recv_at, who):
         return pltpu.make_async_remote_copy(
-            src_ref=part, dst_ref=part, send_sem=mir_send.at[i], recv_sem=mir_recv.at[i],
-            device_id=(mate, lat, lon), device_id_type=MESH,
+            src_ref=src, dst_ref=dst, send_sem=send, recv_sem=recv_at, device_id=who, device_id_type=MESH
         )
 
-    def hop(r):
-        src = stage.at[r] if r else pool.at[core * MEMBERS, :, pl.ds(0, SIDE), :]
-        return pltpu.make_async_remote_copy(
-            src_ref=src, dst_ref=recv.at[core, r], send_sem=z_send.at[r], recv_sem=z_recv.at[r],
-            device_id=(ahead, lat, lon), device_id_type=MESH,
-        )
-
-    def forward(r):
-        return pltpu.make_async_remote_copy(
-            src_ref=recv.at[core, r], dst_ref=recv.at[core, r], send_sem=fwd_send.at[r], recv_sem=fwd_recv.at[r],
-            device_id=(mate, lat, lon), device_id_type=MESH,
-        )
-
-    for copy in halo_a:
+    body = pl.ds(0, SIDE)
+    own_a = [pool_a.at[core * 2 + k, :, body, :] for k in range(2)]
+    own_b = pool_b.at[pl.ds(core * 2, 2), :, body, :]
+    mirrors = [
+        remote(part, part, mir_send.at[i], mir_recv.at[i], (mate, lat, lon))
+        for i, part in enumerate([own_a[0], own_a[1], own_b])
+    ]
+    final = rounds - 1
+    parts = [pl.ds(3 * i, 3) for i in range(3)]
+    hops, forwards = [], []
+    for r in range(final):
+        src, dst = (stage.at[r] if r else own_a[0]), recv.at[core, r]
+        hops.append(remote(src, dst, z_send.at[r], z_recv.at[r], (ahead, lat, lon)))
+        forwards.append(remote(dst, dst, fwd_send.at[r], fwd_recv.at[r], (mate, lat, lon)))
+    for i, part in enumerate(parts):
+        src, dst, at = stage.at[final, part], last.at[core, part], final + i
+        hops.append(remote(src, dst, z_send.at[at], z_recv.at[at], (ahead, lat, lon)))
+        forwards.append(remote(dst, dst, fwd_send.at[at], fwd_recv.at[at], (mate, lat, lon)))
+
+    def send(r):
+        at, relay, which = (plan[PLAN_SENDS + 3 * r + i] for i in range(3))
+
+        def fill(f, _):
+            x = pool_a[at & 3, f, body, :]
+            if r >= 2:
+                x = jnp.where(at >= 4, pool_b[at & 3, f, body, :], x)
+            for q in range(r - 1):
+                x = jnp.where((relay == 1) & (which == q), recv[core, q, f], x)
+            stage[r, f] = x
+            return 0
+
+        if r < final:
+            lax.fori_loop(0, FIELDS, fill, 0)
+            hops[r].start()
+        else:
+            for i in range(3):
+                lax.fori_loop(3 * i, 3 * i + 3, fill, 0)
+                hops[r + i].start()
+
+    for copy in halos[0]:
         copy.wait_recv()
     for i in range(2):
         st[i, pl.ds(SIDE, HALO), :] = st_land[i]
     for j in range(GROUPS):
         wf[j] = st[1, strided(j), :]
     advance(0, (0,))
-    hops = [hop(r) for r in range(rounds)]
-    forwards = [forward(r) for r in range(rounds)]
     hops[0].start()
-    mirrors = [mirror(0, 1, 0), mirror(1, MEMBERS - 1, 1)]
     mirrors[0].start()
-
-    for copy in halo_b:
+    for copy in halos[1]:
         copy.wait_recv()
-    advance(1, (0, 32, 64))
+    advance(1, (0,))
     mirrors[1].start()
-    for copy in mirrors:
+    mirrors[0].wait_recv()
+    mirrors[1].wait_recv()
+    send(1)
+    for copy in halos[2]:
         copy.wait_recv()
-
-    for r in range(1, rounds):
-        if r >= 2:
-            hops[r - 2].wait_recv()
-            forwards[r - 2].start()
-            hops[r - 2].wait_send()
-        own, relay, which = (plan[PLAN_SENDS + 3 * r + i] for i in range(3))
-
-        def fill_stage(f, _):
-            x = pool[own, f, pl.ds(0, SIDE), :]
-            for q in range(r - 1):
-                x = jnp.where((relay == 1) & (which == q), recv[core, q, f], x)
-            stage[r, f] = x
-            return 0
-
-        lax.fori_loop(0, FIELDS, fill_stage, 0)
-        hops[r].start()
-    for r in range(max(0, rounds - 2), rounds):
-        hops[r].wait_recv()
-        forwards[r].start()
-        hops[r].wait_send()
-    for copy in forwards:
-        copy.wait()
-    for copy in mirrors:
-        copy.wait_send()
-    for copy in halo_a + halo_b:
-        copy.wait_send()
-
+    advance(2, (0, 32))
+    mirrors[2].start()
+    mirrors[2].wait_recv()
+    for r in range(2, rounds):
+        hops[r - 2].wait_recv()
+        forwards[r - 2].start()
+        hops[r - 2].wait_send()
+        send(r)
+    hops[final - 1].wait_recv()
+    forwards[final - 1].start()
+    for copy in forwards[:final]:
+        copy.wait_recv()
     writes = []
-    for i in range(MEMBERS):
-        here, at, way, when = (plan[PLAN_OUTS + 4 * i + e] for e in range(4))
-
-        def choose(f, _):
-            done[i, f] = jnp.where(here == 1, pool[at, f, pl.ds(0, SIDE), :], recv[way, when, f])
-            return 0
-
-        lax.fori_loop(0, FIELDS, choose, 0)
-        write = pltpu.make_async_copy(done.at[i], out.at[i], out_sem.at[i])
+    for i, part in enumerate(parts):
+        hops[final + i].wait_recv()
+        forwards[final + i].start()
+        forwards[final + i].wait_recv()
+        for m in range(MEMBERS):
+            here, at, way, when = (plan[PLAN_OUTS + 4 * m + e] for e in range(4))
+
+            def choose(f, _):
+                x = recv[way, jnp.minimum(when, final - 1), f]
+                late = jnp.where(way == 0, last[0, f], last[1, f])
+                x = jnp.where(when == final, late, x)
+                mine = jnp.where(at < 4, pool_a[at & 3, f, body, :], pool_b[at & 3, f, body, :])
+                done[m, f] = jnp.where(here == 1, mine, x)
+                return 0
+
+            lax.fori_loop(3 * i, 3 * i + 3, choose, 0)
+        write = pltpu.make_async_copy(done.at[:, part], out.at[:, part], out_sem.at[i])
         write.start()
         writes.append(write)
     for write in writes:
         write.wait()
+    for copy in hops[final - 1 :] + forwards + mirrors + halos[1] + halos[2]:
+        copy.wait_send()
 
 
 def main_call(rounds, cid):
@@ -558,25 +629,27 @@
         pltpu.VMEM((MEMBERS, FIELDS, HALO, SIDE), f32),
         pltpu.VMEM((MEMBERS, FIELDS, HALO, SIDE), f32),
         pltpu.VMEM((FIELDS, ROWS, SIDE), f32),
-        pltpu.VMEM((3, FIELDS, GROUPS, 8, SIDE), f32),
+        pltpu.VMEM((2, FIELDS, GROUPS, 8, SIDE), f32),
         pltpu.VMEM((FIELDS, GROUPS, 8, SIDE), f32),
-        pltpu.VMEM((3, GROUPS, 8, SIDE), f32),
+        pltpu.VMEM((2, GROUPS, 8, SIDE), f32),
         pltpu.VMEM((GROUPS, 8, SIDE), f32),
         pltpu.VMEM((GROUPS, 8, SIDE), f32),
-        pltpu.VMEM((2 * MEMBERS, FIELDS, ROWS, SIDE), f32),
-        pltpu.VMEM((2, rounds, *tile), f32),
+        pltpu.VMEM((MEMBERS, FIELDS, ROWS, SIDE), f32),
+        pltpu.VMEM((MEMBERS, FIELDS, ROWS, SIDE), f32),
+        pltpu.VMEM((2, rounds - 1, *tile), f32),
+        pltpu.VMEM((2, *tile), f32),
         pltpu.VMEM((rounds, *tile), f32),
         pltpu.VMEM((MEMBERS, *tile), f32),
         pltpu.SemaphoreType.DMA((2,)),
-        pltpu.SemaphoreType.DMA((2, 6)),
-        pltpu.SemaphoreType.DMA((2, 6)),
-        pltpu.SemaphoreType.DMA((2,)),
-        pltpu.SemaphoreType.DMA((2,)),
-        pltpu.SemaphoreType.DMA((rounds,)),
-        pltpu.SemaphoreType.DMA((rounds,)),
-        pltpu.SemaphoreType.DMA((rounds,)),
-        pltpu.SemaphoreType.DMA((rounds,)),
-        pltpu.SemaphoreType.DMA((MEMBERS,)),
+        pltpu.SemaphoreType.DMA((3, 6)),
+        pltpu.SemaphoreType.DMA((3, 6)),
+        pltpu.SemaphoreType.DMA((3,)),
+        pltpu.SemaphoreType.DMA((3,)),
+        pltpu.SemaphoreType.DMA((rounds + 2,)),
+        pltpu.SemaphoreType.DMA((rounds + 2,)),
+        pltpu.SemaphoreType.DMA((rounds + 2,)),
+        pltpu.SemaphoreType.DMA((rounds + 2,)),
+        pltpu.SemaphoreType.DMA((3,)),
     ]
     return pl.pallas_call(
         functools.partial(main_kernel, rounds),
@@ -608,7 +681,7 @@
             pl.BlockSpec(memory_space=pltpu.VMEM),
         ],
         out_specs=(pl.BlockSpec(memory_space=pltpu.SMEM), pl.BlockSpec(memory_space=pltpu.VMEM)),
-        scratch_shapes=[pltpu.SMEM((8 * MOST,), jnp.int32)] * 2,
+        scratch_shapes=[pltpu.SMEM((8 * MOST,), jnp.int32)] * 2 + [pltpu.SMEM((16,), jnp.int32)],
         name="plan",
     )(ancestors, coriolis.reshape(1, SIDE), depth)
 

time: 96.3 us -> 74.4 us (0.77)
  between operations: 13.4 us -> 0.06 us
  Pallas kernels: 81 us -> 68.9 us
  local copies, waits for them, and re-layouts: 1.41 us -> 4.81 us
    pallas_call x1, Pallas kernels: 78.5 us -> 66.6 us  [run(): return main_call(rounds, cid)(plan, flat, stat).reshape(states.shape)]
    unnamed x1 -> x8, local copies, waits for them, and re-layouts: 1.41 us -> 4.81 us
where the time goes in v1:
time: 74.4 us; the launch traced here: 74 us
  Pallas kernels  68.9 us (93%)
  local copies, waits for them, and re-layouts  4.81 us (6%)
    pallas_call x1, Pallas kernels, run(): return main_call(rounds, cid)(plan, flat, stat).reshape(states.shape)  66.6 us
    unnamed x8, local copies, waits for them, and re-layouts  4.81 us
    pallas_call x1, Pallas kernels, body(): pl.pallas_call(plan_kernel, out_shape=(jax.ShapeDtypeStruct((PLAN_SIZE,),...  2.29 us

profile of v1, /device:TPU:1, one launch (start us, length us, event | category | flops | bytes accessed | tf_op | source)
XLA Modules:
  0.0 74.0 jit_solution(12202836065872523677)
XLA Ops:
  0.0 0.0 copy-start.1
  0.0 0.0 copy-start.2
  0.0 0.0 copy-start
  0.0 3.4 %copy.73 = f32[4,3,3,128,128]{4,3,2,1,0:T(8,128)} copy(f32[4,3,3,128,128]{4,3,2,1,0:T(8,128)} %param.12) | data formatting | bytes 4718592
  3.4 0.0 copy-done.1
  3.4 0.0 copy-done.2
  3.4 0.0 copy-done
  3.4 2.3 %plan.1 = (s32[42]{0:T(128)S(1)}, f32[2,128,128]{2,1,0:T(8,128)S(1)}) custom-call(s32[32]{0:T(128)S(1)} %copy-done.2, f32[1,128]{1,0:T(1,128)S(1)} %bitcast.91, f32[128,128]{1,0:T(8,128)S(1)} %copy-done), custom_call_target="tpu_custom_call" | custom-call | tf_op jit(solution)/shard_map/plan/pallas_call | solution.py:672
  5.7 66.9 %conditional.1 = (f32[4,3,3,128,128]{4,3,2,1,0:T(8,128)S(1)}) conditional(s32[]{:T(128)} %bitcast.11, (f32[4,3,3,128,128]{4,3,2,1,0:T(8,128)}, s32[42]{0:T(128)S(1)}, f32[2,128,128]{2,1,0:T(8,128)S(1)}) %tuple.50, (f32[4,3,3,128,128]{4,3,2,1,0:T(8,128)}, s32[42]{0:T(128)S(1)}, ...), branch_computations={%region_0.0_spmd, %region_1.0_spmd, %region_2.0_spmd, %region_3.8_... | conditional | flops 10439263 | bytes 79931488 | solution.py:699
  5.8 66.6 %cycle_5.1 = f32[4,9,128,128]{3,2,1,0:T(8,128)S(1)} custom-call(s32[42]{0:T(128)S(1)} %get-tuple-element.250.plan, f32[4,9,128,128]{3,2,1,0:T(8,128)} %bitcast.2.states, f32[2,128,128]{2,1,0:T(8,128)S(1)} %get-tuple-element.252.stat), custom_call_target="tpu_custom_call" | custom-call | tf_op jit(solution)/shard_map/cond/branch_1_fun/cycle_5/pallas_call | solution.py:691
  72.6 1.4 %copy.74 = f32[4,3,3,128,128]{4,3,2,1,0:T(8,128)} copy(f32[4,3,3,128,128]{4,3,2,1,0:T(8,128)S(1)} %get-tuple-element.340) | data formatting | bytes 4718592
Async XLA Ops:
  0.0 3.4 %copy-start.1 = (f32[128]{0:T(128)S(1)}, f32[128]{0:T(128)}, u32[]{:S(2)}) copy-start(f32[128]{0:T(128)} %param.14) | copy-start | bytes 1540
  0.0 3.4 %copy-start.2 = (s32[32]{0:T(128)S(1)}, s32[32]{0:T(128)}, u32[]{:S(2)}) copy-start(s32[32]{0:T(128)} %anc_ref.1) | copy-start | bytes 388
  0.0 3.4 %copy-start = (f32[128,128]{1,0:T(8,128)S(1)}, f32[128,128]{1,0:T(8,128)}, u32[]{:S(2)}) copy-start(f32[128,128]{1,0:T(8,128)} %depth_ref.1) | copy-start | bytes 196612

commit v2 on v1

--- a/solution.py
+++ b/solution.py
@@ -25,7 +25,8 @@
 ROUNDS = (4, 5, 6)
 MOST = ROUNDS[-1]
 PLAN_SENDS = 8
-PLAN_OUTS = PLAN_SENDS + 3 * MOST
+HALF = SIDE // 2
+PLAN_OUTS = PLAN_SENDS + 6 * MOST
 PLAN_SIZE = PLAN_OUTS + 4 * MEMBERS
 
 
@@ -96,14 +97,12 @@
     wanted = lax.dynamic_slice_in_dim(ancestors, lax.axis_index("particle") * count, count)
     me, devices = lax.axis_index("particle"), lax.axis_size("particle")
 
-    def turn(k, carry):
-        piece, current = carry
-        owner = lax.rem(me - k + devices, devices)
-        here = (wanted // count == owner)[:, None, None, None, None]
+    piece, current = states, jnp.zeros_like(states)
+    for k in range(devices):
+        here = (wanted // count == lax.rem(me - k + devices, devices))[:, None, None, None, None]
         current = jnp.where(here, jnp.take(piece, wanted % count, axis=0, mode="clip"), current)
-        return lax.ppermute(piece, "particle", [(i, (i + 1) % devices) for i in range(devices)]), current
-
-    current = lax.fori_loop(0, devices, turn, (states, jnp.zeros_like(states)))[1]
+        if k < devices - 1:
+            piece = lax.ppermute(piece, "particle", [(i, (i + 1) % devices) for i in range(devices)])
     rows = lax.axis_index("lat") * ny + jnp.arange(ny)
     wall = (rows > 0).astype(jnp.float32)[:, None]
 
@@ -241,16 +240,18 @@
         third = jnp.where((one != down) & (two != down), down, third)
     for k, local in enumerate((one, two, third, fourth)):
         plan_ref[1 + k] = local
-    behind = lax.rem(chip + 3 + 2 * core, 4)
-    for r in range(1, MOST):
-        at = (core * MOST + r) * 4 + chip
-        relay = passed_ref[at]
-        plan_ref[PLAN_SENDS + 3 * r] = pool_of(place8(own_ref[at]))
-        plan_ref[PLAN_SENDS + 3 * r + 1] = jnp.where(relay != 0, 1, 0)
-        found = jnp.int32(0)
-        for q in range(r - 1):
-            found = jnp.where(own_ref[(core * MOST + q) * 4 + behind] == relay, q, found)
-        plan_ref[PLAN_SENDS + 3 * r + 2] = found
+    for d in range(2):
+        behind = lax.rem(chip + 3 + 2 * d, 4)
+        for r in range(1, MOST):
+            at = (d * MOST + r) * 4 + chip
+            relay = passed_ref[at]
+            entry = PLAN_SENDS + 3 * (2 * r + d)
+            plan_ref[entry] = pool_of(place8(own_ref[at]))
+            plan_ref[entry + 1] = jnp.where(relay != 0, 1, 0)
+            found = jnp.int32(0)
+            for q in range(r - 1):
+                found = jnp.where(own_ref[(d * MOST + q) * 4 + behind] == relay, q, found)
+            plan_ref[entry + 2] = found
     for i in range(MEMBERS):
         m = anc_ref[particle * MEMBERS + i]
         bit = m & 7
@@ -276,8 +277,8 @@
 
 def main_kernel(
     rounds, plan, states, stat, out,
-    raw, st, st_edge, st_land, pack_w, pack_e, land_w, land_e, edge, edge_land,
-    tall, wm, ws, wd, wds, wf, pool_a, pool_b, recv, last, stage, done,
+    raw, st, st_edge, st_land, pack_w, pack_e, land_w, land_e, rim_w, rim_e, side_w, side_e, edge, edge_land,
+    tall, wm, ws, wd, wds, wf, pool_a, pool_b, early, recv, last, stage, done,
     in_sem, halo_send, halo_recv, mir_send, mir_recv, z_send, z_recv, fwd_send, fwd_recv, out_sem,
 ):
     particle, lat, lon = lax.axis_index("particle"), lax.axis_index("lat"), lax.axis_index("lon")
@@ -285,8 +286,7 @@
     lat2 = 1 - lat
     east, west = lax.rem(lon + 1, 8), lax.rem(lon + 7, 8)
     mate = chip * 2 + 1 - core
-    ahead = lax.rem(chip + 1 + 2 * core, 4) * 2 + core
-    behind = lax.rem(chip + 3 + 2 * core, 4) * 2 + core
+    above, below = lax.rem(chip + 1, 4) * 2 + core, lax.rem(chip + 3, 4) * 2 + core
 
     load = pltpu.make_async_copy(states, raw, in_sem.at[0])
     load.start()
@@ -295,7 +295,7 @@
     barrier = pltpu.get_barrier_semaphore()
     everyone = (
         (particle, lat, east), (particle, lat, west), (particle, lat2, lon), (particle, lat2, east),
-        (particle, lat2, west), (mate, lat, lon), (ahead, lat, lon), (behind, lat, lon),
+        (particle, lat2, west), (mate, lat, lon), (above, lat, lon), (below, lat, lon),
     )
     for who in everyone:
         pl.semaphore_signal(barrier, inc=1, device_id=who, device_id_type=MESH)
@@ -326,13 +326,12 @@
 
     def halo_copies(first, count, group):
         at = pl.ds(first, count)
-        body, tail = pl.ds(0, SIDE), pl.ds(SIDE, HALO)
         rim = pl.ds(edge_row, HALO)
         ways = [
-            (pack_w.at[at], land_w.at[at, body, :], (particle, lat, east)),
-            (pack_e.at[at], land_e.at[at, body, :], (particle, lat, west)),
-            (pack_w.at[at, rim, :], land_w.at[at, tail, :], (particle, lat2, east)),
-            (pack_e.at[at, rim, :], land_e.at[at, tail, :], (particle, lat2, west)),
+            (pack_w.at[at], land_w.at[at], (particle, lat, east)),
+            (pack_e.at[at], land_e.at[at], (particle, lat, west)),
+            (pack_w.at[at, rim, :], rim_w.at[at], (particle, lat2, east)),
+            (pack_e.at[at, rim, :], rim_e.at[at], (particle, lat2, west)),
             (edge.at[at], edge_land.at[at], (particle, lat2, lon)),
         ]
         if first == 0:
@@ -347,6 +346,11 @@
 
     load_stat.wait()
     load.wait()
+
+    def pack_all(k, _):
+        pack(k)
+        return 0
+
     pack(0)
     for i in range(2):
         st_edge[i] = st[i, pl.ds(edge_row, HALO), :]
@@ -355,11 +359,7 @@
     for copy in halos[0]:
         copy.start()
 
-    def pack_more(k, _):
-        pack(k)
-        return 0
-
-    lax.fori_loop(1, MEMBERS, pack_more, 0)
+    lax.fori_loop(1, MEMBERS, pack_all, 0)
     for copy in halos[0]:
         copy.wait_send()
     for copy in halos[1] + halos[2]:
@@ -381,7 +381,7 @@
     no_north = (sub == 7) & (lat == 1)
     wall = (sub == 0) & (lat == 0)
 
-    def advance(first, offs):
+    def advance(first, offs, between, after):
         n = len(offs)
         tiles = range(n + 1)
 
@@ -397,14 +397,20 @@
                     wm[g, f, j] = pltpu.roll(x, off, 1) if off else x
                 return 0
 
-            lax.fori_loop(0, FIELDS, fill, 0)
+            lax.fori_loop(0, FIELDS, fill, 0, unroll=3 if off else 1)
             for j in range(GROUPS):
                 x = st[0, strided(j), :]
                 wd[g, j] = pltpu.roll(x, off, 1) if off else x
 
+        for g in range(n):
+            side_w[g, pl.ds(0, SIDE), :] = land_w[first + g]
+            side_e[g, pl.ds(0, SIDE), :] = land_e[first + g]
+            side_w[g, pl.ds(SIDE, HALO), :] = rim_w[first + g]
+            side_e[g, pl.ds(SIDE, HALO), :] = rim_e[first + g]
+
         def fill_strip(j, _):
-            lw = [land_w[first + g, strided(j), :] for g in range(n)]
-            le = [land_e[first + g, strided(j), :] for g in range(n)]
+            lw = [side_w[g, strided(j), :] for g in range(n)]
+            le = [side_e[g, strided(j), :] for g in range(n)]
             for f in range(FIELDS + 1):
                 total = None
                 for g, off in enumerate(offs):
@@ -418,7 +424,10 @@
                     wds[j] = total
             return 0
 
-        lax.fori_loop(0, GROUPS, fill_strip, 0)
+        for j in range(GROUPS):
+            fill_strip(j, 0)
+
+        between()
 
         def get(f, j):
             return [wm[g, f, j] for g in range(n)] + [ws[f, j]]
@@ -509,54 +518,77 @@
             def drain(f, _):
                 for j in range(GROUPS):
                     x = wm[g, f, j]
-                    pool[slot, f, strided(j), :] = pltpu.roll(x, SIDE - off, 1) if off else x
+                    tall[f, strided(j), :] = pltpu.roll(x, SIDE - off, 1) if off else x
+                for half in range(2):
+                    pool[slot, half, f] = tall[f, pl.ds(HALF * half, HALF), :]
                 return 0
 
-            lax.fori_loop(0, FIELDS, drain, 0)
+            lax.fori_loop(0, FIELDS, drain, 0, unroll=3 if off else 1)
+            after[g]()
 
     def remote(src, dst, send, recv_at, who):
         return pltpu.make_async_remote_copy(
             src_ref=src, dst_ref=dst, send_sem=send, recv_sem=recv_at, device_id=who, device_id_type=MESH
         )
 
-    body = pl.ds(0, SIDE)
-    own_a = [pool_a.at[core * 2 + k, :, body, :] for k in range(2)]
-    own_b = pool_b.at[pl.ds(core * 2, 2), :, body, :]
+    ways = (core, 1 - core)
+    aims = ((lax.rem(chip + 1 + 2 * core, 4) * 2 + core, lat, lon), (lax.rem(chip + 3 - 2 * core, 4) * 2 + core, lat, lon))
+    firsts = [pool_a.at[core * 2 + k] for k in range(2)]
     mirrors = [
         remote(part, part, mir_send.at[i], mir_recv.at[i], (mate, lat, lon))
-        for i, part in enumerate([own_a[0], own_a[1], own_b])
+        for i, part in enumerate([*firsts, pool_b.at[core * 2], pool_b.at[core * 2 + 1]])
     ]
     final = rounds - 1
     parts = [pl.ds(3 * i, 3) for i in range(3)]
     hops, forwards = [], []
     for r in range(final):
-        src, dst = (stage.at[r] if r else own_a[0]), recv.at[core, r]
-        hops.append(remote(src, dst, z_send.at[r], z_recv.at[r], (ahead, lat, lon)))
+        if r == 0:
+            dst = early.at[core]
+            hops.append([remote(pool_a.at[core * 2], dst, z_send.at[0, 0], z_recv.at[0, 0], aims[0])])
+        else:
+            pair = []
+            for e in range(2):
+                dst = recv.at[r - 1, core, ways[e]]
+                pair.append(remote(stage.at[r, e], dst, z_send.at[r, e], z_recv.at[r, e], aims[e]))
+            hops.append(pair)
+            dst = recv.at[r - 1, core]
         forwards.append(remote(dst, dst, fwd_send.at[r], fwd_recv.at[r], (mate, lat, lon)))
     for i, part in enumerate(parts):
-        src, dst, at = stage.at[final, part], last.at[core, part], final + i
-        hops.append(remote(src, dst, z_send.at[at], z_recv.at[at], (ahead, lat, lon)))
+        at = final + i
+        hops.append(
+            [
+                remote(stage.at[final, e, part], last.at[i, core, ways[e]], z_send.at[at, e], z_recv.at[at, e], aims[e])
+                for e in range(2)
+            ]
+        )
+        dst = last.at[i, core]
         forwards.append(remote(dst, dst, fwd_send.at[at], fwd_recv.at[at], (mate, lat, lon)))
 
     def send(r):
-        at, relay, which = (plan[PLAN_SENDS + 3 * r + i] for i in range(3))
+        picks = [[plan[PLAN_SENDS + 3 * (2 * r + way) + i] for i in range(3)] for way in ways]
 
         def fill(f, _):
-            x = pool_a[at & 3, f, body, :]
-            if r >= 2:
-                x = jnp.where(at >= 4, pool_b[at & 3, f, body, :], x)
-            for q in range(r - 1):
-                x = jnp.where((relay == 1) & (which == q), recv[core, q, f], x)
-            stage[r, f] = x
+            for e in range(2):
+                at, relay, which = picks[e]
+                x = pool_a[at & 3, core, f]
+                if r >= 2:
+                    x = jnp.where(at >= 4, pool_b[at & 3, core, f], x)
+                for q in range(r - 1):
+                    y = recv[q - 1, core, ways[e], f] if q else early[ways[e], core, f]
+                    x = jnp.where((relay == 1) & (which == q), y, x)
+                stage[r, e, f] = x
             return 0
 
-        if r < final:
-            lax.fori_loop(0, FIELDS, fill, 0)
-            hops[r].start()
-        else:
-            for i in range(3):
-                lax.fori_loop(3 * i, 3 * i + 3, fill, 0)
-                hops[r + i].start()
+        pieces = [(0, FIELDS)] if r < final else [(3 * i, 3 * i + 3) for i in range(3)]
+        for i, (low, high) in enumerate(pieces):
+            lax.fori_loop(low, high, fill, 0)
+            for copy in hops[r + i]:
+                copy.start()
+
+    def arrive(r):
+        for copy in hops[r]:
+            copy.wait_recv()
+        forwards[r].start()
 
     for copy in halos[0]:
         copy.wait_recv()
@@ -564,44 +596,48 @@
         st[i, pl.ds(SIDE, HALO), :] = st_land[i]
     for j in range(GROUPS):
         wf[j] = st[1, strided(j), :]
-    advance(0, (0,))
-    hops[0].start()
-    mirrors[0].start()
+    def nothing():
+        pass
+
+    def second():
+        mirrors[0].wait_recv()
+        mirrors[1].wait_recv()
+        send(1)
+
+    advance(0, (0,), nothing, [lambda: (hops[0][0].start(), mirrors[0].start())])
     for copy in halos[1]:
         copy.wait_recv()
-    advance(1, (0,))
-    mirrors[1].start()
-    mirrors[0].wait_recv()
-    mirrors[1].wait_recv()
-    send(1)
+    advance(1, (0,), nothing, [mirrors[1].start])
     for copy in halos[2]:
         copy.wait_recv()
-    advance(2, (0, 32))
-    mirrors[2].start()
+    advance(2, (0, 32), second, [mirrors[2].start, mirrors[3].start])
     mirrors[2].wait_recv()
+    mirrors[3].wait_recv()
     for r in range(2, rounds):
-        hops[r - 2].wait_recv()
-        forwards[r - 2].start()
-        hops[r - 2].wait_send()
+        arrive(r - 2)
+        for copy in hops[r - 2]:
+            copy.wait_send()
+        if r == 2:
+            forwards[0].wait_recv()
         send(r)
-    hops[final - 1].wait_recv()
-    forwards[final - 1].start()
-    for copy in forwards[:final]:
+    arrive(final - 1)
+    for copy in forwards[1:final]:
         copy.wait_recv()
     writes = []
     for i, part in enumerate(parts):
-        hops[final + i].wait_recv()
-        forwards[final + i].start()
+        arrive(final + i)
         forwards[final + i].wait_recv()
         for m in range(MEMBERS):
             here, at, way, when = (plan[PLAN_OUTS + 4 * m + e] for e in range(4))
 
             def choose(f, _):
-                x = recv[way, jnp.minimum(when, final - 1), f]
-                late = jnp.where(way == 0, last[0, f], last[1, f])
-                x = jnp.where(when == final, late, x)
-                mine = jnp.where(at < 4, pool_a[at & 3, f, body, :], pool_b[at & 3, f, body, :])
-                done[m, f] = jnp.where(here == 1, mine, x)
+                for half in range(2):
+                    x = recv[jnp.clip(when - 1, 0, final - 2), half, way, f]
+                    x = jnp.where(when == 0, early[way, half, f], x)
+                    late = jnp.where(way == 0, last[i, half, 0, f - 3 * i], last[i, half, 1, f - 3 * i])
+                    x = jnp.where(when == final, late, x)
+                    local = jnp.where(at < 4, pool_a[at & 3, half, f], pool_b[at & 3, half, f])
+                    done[m, f, pl.ds(HALF * half, HALF), :] = jnp.where(here == 1, local, x)
                 return 0
 
             lax.fori_loop(3 * i, 3 * i + 3, choose, 0)
@@ -610,7 +646,7 @@
         writes.append(write)
     for write in writes:
         write.wait()
-    for copy in hops[final - 1 :] + forwards + mirrors + halos[1] + halos[2]:
+    for copy in [copy for pair in hops[final - 1 :] for copy in pair] + forwards + mirrors + halos[1] + halos[2]:
         copy.wait_send()
 
 
@@ -624,8 +660,12 @@
         pltpu.VMEM((2, HALO, SIDE), f32),
         pltpu.VMEM((MEMBERS, SIDE, SIDE), f32),
         pltpu.VMEM((MEMBERS, SIDE, SIDE), f32),
-        pltpu.VMEM((MEMBERS, ROWS, SIDE), f32),
-        pltpu.VMEM((MEMBERS, ROWS, SIDE), f32),
+        pltpu.VMEM((MEMBERS, SIDE, SIDE), f32),
+        pltpu.VMEM((MEMBERS, SIDE, SIDE), f32),
+        pltpu.VMEM((MEMBERS, HALO, SIDE), f32),
+        pltpu.VMEM((MEMBERS, HALO, SIDE), f32),
+        pltpu.VMEM((2, ROWS, SIDE), f32),
+        pltpu.VMEM((2, ROWS, SIDE), f32),
         pltpu.VMEM((MEMBERS, FIELDS, HALO, SIDE), f32),
         pltpu.VMEM((MEMBERS, FIELDS, HALO, SIDE), f32),
         pltpu.VMEM((FIELDS, ROWS, SIDE), f32),
@@ -634,19 +674,20 @@
         pltpu.VMEM((2, GROUPS, 8, SIDE), f32),
         pltpu.VMEM((GROUPS, 8, SIDE), f32),
         pltpu.VMEM((GROUPS, 8, SIDE), f32),
-        pltpu.VMEM((MEMBERS, FIELDS, ROWS, SIDE), f32),
-        pltpu.VMEM((MEMBERS, FIELDS, ROWS, SIDE), f32),
-        pltpu.VMEM((2, rounds - 1, *tile), f32),
-        pltpu.VMEM((2, *tile), f32),
-        pltpu.VMEM((rounds, *tile), f32),
+        pltpu.VMEM((MEMBERS, 2, FIELDS, HALF, SIDE), f32),
+        pltpu.VMEM((MEMBERS, 2, FIELDS, HALF, SIDE), f32),
+        pltpu.VMEM((2, 2, FIELDS, HALF, SIDE), f32),
+        pltpu.VMEM((rounds - 2, 2, 2, FIELDS, HALF, SIDE), f32),
+        pltpu.VMEM((3, 2, 2, 3, HALF, SIDE), f32),
+        pltpu.VMEM((rounds, 2, FIELDS, HALF, SIDE), f32),
         pltpu.VMEM((MEMBERS, *tile), f32),
         pltpu.SemaphoreType.DMA((2,)),
         pltpu.SemaphoreType.DMA((3, 6)),
         pltpu.SemaphoreType.DMA((3, 6)),
-        pltpu.SemaphoreType.DMA((3,)),
-        pltpu.SemaphoreType.DMA((3,)),
-        pltpu.SemaphoreType.DMA((rounds + 2,)),
-        pltpu.SemaphoreType.DMA((rounds + 2,)),
+        pltpu.SemaphoreType.DMA((4,)),
+        pltpu.SemaphoreType.DMA((4,)),
+        pltpu.SemaphoreType.DMA((rounds + 2, 2)),
+        pltpu.SemaphoreType.DMA((rounds + 2, 2)),
         pltpu.SemaphoreType.DMA((rounds + 2,)),
         pltpu.SemaphoreType.DMA((rounds + 2,)),
         pltpu.SemaphoreType.DMA((3,)),

time: 74.4 us -> 60.5 us (0.81)
  Pallas kernels: 68.9 us -> 58.4 us
  local copies, waits for them, and re-layouts: 4.81 us -> 1.41 us
    pallas_call x1, Pallas kernels: 66.6 us -> 55.7 us  [run(): return main_call(rounds, cid)(plan, flat, stat).reshape(states.shape)]
    unnamed x8 -> x1, local copies, waits for them, and re-layouts: 4.81 us -> 1.41 us
where the time goes in v2:
time: 60.5 us; the launch traced here: 60.1 us
  Pallas kernels  58.4 us (97%)
  local copies, waits for them, and re-layouts  1.41 us (2%)
    pallas_call x1, Pallas kernels, run(): return main_call(rounds, cid)(plan, flat, stat).reshape(states.shape)  55.7 us
    pallas_call x1, Pallas kernels, body(): pl.pallas_call(plan_kernel, out_shape=(jax.ShapeDtypeStruct((PLAN_SIZE,),...  2.67 us
    unnamed x1, local copies, waits for them, and re-layouts  1.41 us

profile of v2, /device:TPU:1, one launch (start us, length us, event | category | flops | bytes accessed | tf_op | source)
XLA Modules:
  0.0 60.1 jit_solution(8315777354691089745)
XLA Ops:
  0.0 2.7 %plan.1 = (s32[60]{0:T(128)S(1)}, f32[2,128,128]{2,1,0:T(8,128)S(1)}) custom-call(s32[32]{0:T(128)} %anc_ref.1, f32[1,128]{1,0:T(1,128)} %bitcast.62, f32[128,128]{1,0:T(8,128)} %depth_ref.1), custom_call_target="tpu_custom_call" | custom-call | tf_op jit(solution)/shard_map/plan/pallas_call | solution.py:713
  2.7 56.0 %conditional.1 = (f32[4,3,3,128,128]{4,3,2,1,0:T(8,128)S(1)}) conditional(s32[]{:T(128)} %bitcast.8, (f32[4,3,3,128,128]{4,3,2,1,0:T(8,128)}, s32[60]{0:T(128)S(1)}, f32[2,128,128]{2,1,0:T(8,128)S(1)}) %tuple.21, (f32[4,3,3,128,128]{4,3,2,1,0:T(8,128)}, s32[60]{0:T(128)S(1)}, f32[2,128,128]{2,1,0:T(8,128)S(1)}) %tuple.21, ...), branch_computations={%region_0.0_spmd, %region_1.0_spmd, %region_2.0_spmd, %region_3.6_... | conditional | flops 13978256 | bytes 226470912 | solution.py:740
  2.7 55.7 %cycle_4.1 = f32[4,9,128,128]{3,2,1,0:T(8,128)S(1)} custom-call(s32[60]{0:T(128)S(1)} %get-tuple-element.50.plan, f32[4,9,128,128]{3,2,1,0:T(8,128)} %bitcast.52, f32[2,128,128]{2,1,0:T(8,128)S(1)} %get-tuple-element.54.stat), custom_call_target="tpu_custom_call" | custom-call | tf_op jit(solution)/shard_map/cond/branch_0_fun/cycle_4/pallas_call | solution.py:732
  58.7 1.4 %copy.62 = f32[4,3,3,128,128]{4,3,2,1,0:T(8,128)} copy(f32[4,3,3,128,128]{4,3,2,1,0:T(8,128)S(1)} %get-tuple-element.104) | data formatting | bytes 4718592

commit v3 on v2

--- a/solution.py
+++ b/solution.py
@@ -22,6 +22,9 @@
 ROWS = SIDE + HALO
 GROUPS = ROWS // 8
 WAVES = ((0, 1), (1, 1), (2, 2))
+TILES = len(WAVES)
+DEPTH_AT = (0, FIELDS)
+LEAD = 4
 ROUNDS = (4, 5, 6)
 MOST = ROUNDS[-1]
 PLAN_SENDS = 8
@@ -275,11 +278,18 @@
     stat_ref[1] = jnp.transpose(jnp.broadcast_to((DT * 0.25) * cor_ref[...], (SIDE, SIDE)))
 
 
+def place(slot, field):
+    if slot < 2:
+        return slot, field
+    at = (slot - 2) * FIELDS + field
+    return (2, at) if at < 16 else (1, FIELDS + at - 16)
+
+
 def main_kernel(
     rounds, plan, states, stat, out,
     raw, st, st_edge, st_land, pack_w, pack_e, land_w, land_e, rim_w, rim_e, side_w, side_e, edge, edge_land,
-    tall, wm, ws, wd, wds, wf, pool_a, pool_b, early, recv, last, stage, done,
-    in_sem, halo_send, halo_recv, mir_send, mir_recv, z_send, z_recv, fwd_send, fwd_recv, out_sem,
+    tall, wm, ws, wd, wds, wf, pool_a, pool_b, early, recv, last, stage,
+    in_sem, halo_send, halo_recv, mir_send, mir_recv, z_send, z_recv, fwd_send, fwd_recv,
 ):
     particle, lat, lon = lax.axis_index("particle"), lax.axis_index("lat"), lax.axis_index("lon")
     chip, core = particle // 2, lax.rem(particle, 2)
@@ -304,34 +314,40 @@
     sub = lax.broadcasted_iota(jnp.int32, (8, SIDE), 0)
     edge_row = pl.multiple_of((SIDE - HALO) * lat2, HALO)
 
-    def pack(k):
-        m = plan[1 + k]
+    def pack(tile):
+        held = [(plan[1 + k], f, place(k, f)[1]) for k in range(MEMBERS) for f in range(FIELDS) if place(k, f)[0] == tile]
+        if tile == DEPTH_AT[0]:
+            held.append((None, 0, DEPTH_AT[1]))
 
         def rows(i, _):
             at = pl.multiple_of(i * 8, 8)
             to_e = jnp.zeros((8, SIDE), jnp.float32)
             to_w = jnp.zeros((8, SIDE), jnp.float32)
-            for f in range(FIELDS + 1):
-                x = raw[m, f, pl.ds(at, 8), :] if f < FIELDS else st[0, pl.ds(at, 8), :]
-                x = pltpu.roll(x, 8 * f + 8, 1)
-                to_e = jnp.where((lane >= 8 * f) & (lane < 8 * f + 8), x, to_e)
-                to_w = jnp.where((lane >= 8 * f + 8) & (lane < 8 * f + 16), x, to_w)
-            pack_w[k, pl.ds(at, 8), :] = to_e
-            pack_e[k, pl.ds(at, 8), :] = to_w
+            for m, f, q in held:
+                x = st[0, pl.ds(at, 8), :] if m is None else raw[m, f, pl.ds(at, 8), :]
+                turn = (8 * q + 8) % SIDE
+                x = pltpu.roll(x, turn, 1) if turn else x
+                to_e = jnp.where((lane >= 8 * q) & (lane < 8 * q + 8), x, to_e)
+                to_w = jnp.where((lane >= turn) & (lane < turn + 8), x, to_w)
+            pack_w[tile, pl.ds(at, 8), :] = to_e
+            pack_e[tile, pl.ds(at, 8), :] = to_w
             return 0
 
         lax.fori_loop(0, SIDE // 8, rows, 0)
-        for f in range(FIELDS):
-            edge[k, f] = raw[m, f, pl.ds(edge_row, HALO), :]
+        first, count = WAVES[tile]
+        for k in range(first, first + count):
+            for f in range(FIELDS):
+                edge[k, f] = raw[plan[1 + k], f, pl.ds(edge_row, HALO), :]
 
     def halo_copies(first, count, group):
         at = pl.ds(first, count)
+        cut = pl.ds(group, 1)
         rim = pl.ds(edge_row, HALO)
         ways = [
-            (pack_w.at[at], land_w.at[at], (particle, lat, east)),
-            (pack_e.at[at], land_e.at[at], (particle, lat, west)),
-            (pack_w.at[at, rim, :], rim_w.at[at], (particle, lat2, east)),
-            (pack_e.at[at, rim, :], rim_e.at[at], (particle, lat2, west)),
+            (pack_w.at[cut], land_w.at[cut], (particle, lat, east)),
+            (pack_e.at[cut], land_e.at[cut], (particle, lat, west)),
+            (pack_w.at[cut, rim, :], rim_w.at[cut], (particle, lat2, east)),
+            (pack_e.at[cut, rim, :], rim_e.at[cut], (particle, lat2, west)),
             (edge.at[at], edge_land.at[at], (particle, lat2, lon)),
         ]
         if first == 0:
@@ -347,10 +363,6 @@
     load_stat.wait()
     load.wait()
 
-    def pack_all(k, _):
-        pack(k)
-        return 0
-
     pack(0)
     for i in range(2):
         st_edge[i] = st[i, pl.ds(edge_row, HALO), :]
@@ -359,7 +371,8 @@
     for copy in halos[0]:
         copy.start()
 
-    lax.fori_loop(1, MEMBERS, pack_all, 0)
+    for i in range(1, TILES):
+        pack(i)
     for copy in halos[0]:
         copy.wait_send()
     for copy in halos[1] + halos[2]:
@@ -402,20 +415,21 @@
                 x = st[0, strided(j), :]
                 wd[g, j] = pltpu.roll(x, off, 1) if off else x
 
-        for g in range(n):
-            side_w[g, pl.ds(0, SIDE), :] = land_w[first + g]
-            side_e[g, pl.ds(0, SIDE), :] = land_e[first + g]
-            side_w[g, pl.ds(SIDE, HALO), :] = rim_w[first + g]
-            side_e[g, pl.ds(SIDE, HALO), :] = rim_e[first + g]
+        tile = WAVES.index((first, n))
+        side_w[tile, pl.ds(0, SIDE), :] = land_w[tile]
+        side_e[tile, pl.ds(0, SIDE), :] = land_e[tile]
+        side_w[tile, pl.ds(SIDE, HALO), :] = rim_w[tile]
+        side_e[tile, pl.ds(SIDE, HALO), :] = rim_e[tile]
 
         def fill_strip(j, _):
-            lw = [side_w[g, strided(j), :] for g in range(n)]
-            le = [side_e[g, strided(j), :] for g in range(n)]
+            lw = [side_w[i, strided(j), :] for i in range(tile + 1)]
+            le = [side_e[i, strided(j), :] for i in range(tile + 1)]
             for f in range(FIELDS + 1):
                 total = None
                 for g, off in enumerate(offs):
-                    x = jnp.where((lane >= 8 * f) & (lane < 8 * f + 8), lw[g], le[g])
-                    turn = (off - 8 - 8 * f) % SIDE
+                    i, q = place(first + g, f) if f < FIELDS else DEPTH_AT
+                    x = jnp.where((lane >= 8 * q) & (lane < 8 * q + 8), lw[i], le[i])
+                    turn = (off - 8 - 8 * q) % SIDE
                     x = pltpu.roll(x, turn, 1) if turn else x
                     total = x if g == 0 else jnp.where((lane >= off - 16) & (lane < off + 16), x, total)
                 if f < FIELDS:
@@ -491,11 +505,11 @@
 
         def step(_, carry):
             order = [GROUPS - 1] + list(range(GROUPS - 1))
-            right = {i: easts(order[i]) for i in range(2)}
+            right = {i: easts(order[i]) for i in range(LEAD)}
             made = {}
             for i in range(GROUPS + 1):
-                if i + 2 < GROUPS:
-                    right[i + 2] = easts(order[i + 2])
+                if i + LEAD < GROUPS:
+                    right[i + LEAD] = easts(order[i + LEAD])
                 if i < GROUPS:
                     made[i] = middle(order[i], right.pop(i))
                 if i == 0:
@@ -604,7 +618,7 @@
         mirrors[1].wait_recv()
         send(1)
 
-    advance(0, (0,), nothing, [lambda: (hops[0][0].start(), mirrors[0].start())])
+    advance(0, (0,), nothing, [lambda: (mirrors[0].start(), hops[0][0].start())])
     for copy in halos[1]:
         copy.wait_recv()
     advance(1, (0,), nothing, [mirrors[1].start])
@@ -623,7 +637,6 @@
     arrive(final - 1)
     for copy in forwards[1:final]:
         copy.wait_recv()
-    writes = []
     for i, part in enumerate(parts):
         arrive(final + i)
         forwards[final + i].wait_recv()
@@ -637,15 +650,10 @@
                     late = jnp.where(way == 0, last[i, half, 0, f - 3 * i], last[i, half, 1, f - 3 * i])
                     x = jnp.where(when == final, late, x)
                     local = jnp.where(at < 4, pool_a[at & 3, half, f], pool_b[at & 3, half, f])
-                    done[m, f, pl.ds(HALF * half, HALF), :] = jnp.where(here == 1, local, x)
+                    out[m, f, pl.ds(HALF * half, HALF), :] = jnp.where(here == 1, local, x)
                 return 0
 
             lax.fori_loop(3 * i, 3 * i + 3, choose, 0)
-        write = pltpu.make_async_copy(done.at[:, part], out.at[:, part], out_sem.at[i])
-        write.start()
-        writes.append(write)
-    for write in writes:
-        write.wait()
     for copy in [copy for pair in hops[final - 1 :] for copy in pair] + forwards + mirrors + halos[1] + halos[2]:
         copy.wait_send()
 
@@ -658,14 +666,14 @@
         pltpu.VMEM((2, ROWS, SIDE), f32),
         pltpu.VMEM((2, HALO, SIDE), f32),
         pltpu.VMEM((2, HALO, SIDE), f32),
-        pltpu.VMEM((MEMBERS, SIDE, SIDE), f32),
-        pltpu.VMEM((MEMBERS, SIDE, SIDE), f32),
-        pltpu.VMEM((MEMBERS, SIDE, SIDE), f32),
-        pltpu.VMEM((MEMBERS, SIDE, SIDE), f32),
-        pltpu.VMEM((MEMBERS, HALO, SIDE), f32),
-        pltpu.VMEM((MEMBERS, HALO, SIDE), f32),
-        pltpu.VMEM((2, ROWS, SIDE), f32),
-        pltpu.VMEM((2, ROWS, SIDE), f32),
+        pltpu.VMEM((TILES, SIDE, SIDE), f32),
+        pltpu.VMEM((TILES, SIDE, SIDE), f32),
+        pltpu.VMEM((TILES, SIDE, SIDE), f32),
+        pltpu.VMEM((TILES, SIDE, SIDE), f32),
+        pltpu.VMEM((TILES, HALO, SIDE), f32),
+        pltpu.VMEM((TILES, HALO, SIDE), f32),
+        pltpu.VMEM((TILES, ROWS, SIDE), f32),
+        pltpu.VMEM((TILES, ROWS, SIDE), f32),
         pltpu.VMEM((MEMBERS, FIELDS, HALO, SIDE), f32),
         pltpu.VMEM((MEMBERS, FIELDS, HALO, SIDE), f32),
         pltpu.VMEM((FIELDS, ROWS, SIDE), f32),
@@ -680,7 +688,6 @@
         pltpu.VMEM((rounds - 2, 2, 2, FIELDS, HALF, SIDE), f32),
         pltpu.VMEM((3, 2, 2, 3, HALF, SIDE), f32),
         pltpu.VMEM((rounds, 2, FIELDS, HALF, SIDE), f32),
-        pltpu.VMEM((MEMBERS, *tile), f32),
         pltpu.SemaphoreType.DMA((2,)),
         pltpu.SemaphoreType.DMA((3, 6)),
         pltpu.SemaphoreType.DMA((3, 6)),
@@ -690,7 +697,6 @@
         pltpu.SemaphoreType.DMA((rounds + 2, 2)),
         pltpu.SemaphoreType.DMA((rounds + 2,)),
         pltpu.SemaphoreType.DMA((rounds + 2,)),
-        pltpu.SemaphoreType.DMA((3,)),
     ]
     return pl.pallas_call(
         functools.partial(main_kernel, rounds),
@@ -700,7 +706,7 @@
             pl.BlockSpec(memory_space=pl.ANY),
             pl.BlockSpec(memory_space=pl.ANY),
         ],
-        out_specs=pl.BlockSpec(memory_space=pl.ANY),
+        out_specs=pl.BlockSpec(memory_space=pltpu.VMEM),
         scratch_shapes=scratch,
         compiler_params=pltpu.CompilerParams(
             collective_id=cid, has_side_effects=True, vmem_limit_bytes=50 * 2**20

time: 60.5 us -> 58.8 us (0.972)
  Pallas kernels: 58.4 us -> 56.9 us
    pallas_call x1, Pallas kernels: 55.7 us -> 54.3 us  [run(): return main_call(rounds, cid)(plan, flat, stat).reshape(states.shape)]
where the time goes in v3:
time: 58.8 us; the launch traced here: 58.6 us
  Pallas kernels  56.9 us (97%)
  local copies, waits for them, and re-layouts  1.41 us (2%)
    pallas_call x1, Pallas kernels, run(): return main_call(rounds, cid)(plan, flat, stat).reshape(states.shape)  54.3 us
    pallas_call x1, Pallas kernels, body(): pl.pallas_call(plan_kernel, out_shape=(jax.ShapeDtypeStruct((PLAN_SIZE,),...  2.67 us
    unnamed x1, local copies, waits for them, and re-layouts  1.41 us

profile of v3, /device:TPU:1, one launch (start us, length us, event | category | flops | bytes accessed | tf_op | source)
XLA Modules:
  0.0 58.6 jit_solution(9491791699694544491)
XLA Ops:
  0.0 2.7 %plan.1 = (s32[60]{0:T(128)S(1)}, f32[2,128,128]{2,1,0:T(8,128)S(1)}) custom-call(s32[32]{0:T(128)} %anc_ref.1, f32[1,128]{1,0:T(1,128)} %bitcast.62, f32[128,128]{1,0:T(8,128)} %depth_ref.1), custom_call_target="tpu_custom_call" | custom-call | tf_op jit(solution)/shard_map/plan/pallas_call | solution.py:719
  2.7 54.5 %conditional.1 = (f32[4,3,3,128,128]{4,3,2,1,0:T(8,128)S(1)}) conditional(s32[]{:T(128)} %bitcast.8, (f32[4,3,3,128,128]{4,3,2,1,0:T(8,128)}, s32[60]{0:T(128)S(1)}, f32[2,128,128]{2,1,0:T(8,128)S(1)}) %tuple.21, (f32[4,3,3,128,128]{4,3,2,1,0:T(8,128)}, s32[60]{0:T(128)S(1)}, f32[2,128,128]{2,1,0:T(8,128)S(1)}) %tuple.21, ...), branch_computations={%region_0.0_spmd, %region_1.0_spmd, %region_2.0_spmd, %region_3.6_... | conditional | flops 13978256 | bytes 226470912 | solution.py:746
  2.7 54.3 %cycle_4.1 = f32[4,9,128,128]{3,2,1,0:T(8,128)S(1)} custom-call(s32[60]{0:T(128)S(1)} %get-tuple-element.50.plan, f32[4,9,128,128]{3,2,1,0:T(8,128)} %bitcast.52, f32[2,128,128]{2,1,0:T(8,128)S(1)} %get-tuple-element.54.stat), custom_call_target="tpu_custom_call" | custom-call | tf_op jit(solution)/shard_map/cond/branch_0_fun/cycle_4/pallas_call | solution.py:738
  57.2 1.4 %copy.62 = f32[4,3,3,128,128]{4,3,2,1,0:T(8,128)} copy(f32[4,3,3,128,128]{4,3,2,1,0:T(8,128)S(1)} %get-tuple-element.104) | data formatting | bytes 4718592
